TPU v7x, 128 devices: a whole 4x4x4 slice. The times are simulated.
128 devices in a mesh: row: 16 (over z, y_hi, core), col: 8 (over x, y_lo).
Axes of the slice: x: 4, y: 4 (y_hi: 2, y_lo: 2; y = y_hi * 2 + y_lo), z: 4, core: 2. Of those that a mesh axis runs over, the one named last changes fastest.
Arguments:
- inverse_tiles: bfloat16 [24576, 24576], P('row', 'col'), may hold values from -6 to 6
- factor: bfloat16 [24576, 2048], P('row', 'col'), may hold values from -0.0390625 to 0.0390625
- block_mask: int32 [192, 16], replicated, may hold values 0 or 1
- diag_inverse: float32 [16, 128, 128], replicated, may hold values from -6 to 6
Outputs:
- off_block: bfloat16 [2048, 24576], P('col', 'row')
- diag_block: float32 [16, 128, 128], P('col')
All inputs are finite; a program needn't handle non-finite values.
Results may differ from a plain program's by a relative error of at most 0.012.
Values may be sent and summed in bfloat16 or wider, within the bound.
A program may use at most 128 MiB of HBM per device.

v0:
```python
import jax
import jax.numpy as jnp
from jax import lax
from jax.sharding import Mesh
from jax.sharding import PartitionSpec as P

COL = ("col_0", "col_1")


def whole_of(x, axes, dim):
    for axis in reversed(axes):
        x = lax.all_gather(x, axis, axis=dim, tiled=True)
    return x


def filled_up(lines, length):
    spare = -lines.shape[0] % length
    if not spare:
        return lines
    return jnp.concatenate([lines, jnp.zeros((spare, *lines.shape[1:]), lines.dtype)])


def broadcast_by_parts(x, axis, root):
    lines = jnp.where(lax.axis_index(axis) == root, x, jnp.zeros_like(x)).reshape(
        -1, *x.shape[1:][-1:]
    )
    padded = filled_up(lines, lax.axis_size(axis))
    own = lax.psum_scatter(padded, axis, scatter_dimension=0, tiled=True)
    return lax.all_gather(own, axis, axis=0, tiled=True)[: len(lines)].reshape(x.shape)


def sum_by_axis(x, axes, dim):
    if not axes:
        return x
    nearer = lax.psum_scatter(x, axes[0], scatter_dimension=dim, tiled=True)
    return sum_by_axis(nearer, axes[1:], dim)


def sent_to_all(x, axis):
    length = lax.axis_size(axis)
    return lax.all_to_all(jnp.broadcast_to(x[None], (length, *x.shape)), axis, 0, 0, tiled=True)


def taken_together(x, axis):
    return sent_to_all(x, axis).astype(jnp.float32).sum(axis=0)


def per_device(inverse_tiles, factor, block_mask, diag_inverse):
    rows_here, cols_here = factor.shape
    block_width = diag_inverse.shape[1]
    sup_here = cols_here // block_width
    blocks_here = rows_here // block_width
    row_index = lax.axis_index("row")
    col_index = lax.axis_index(COL)
    mask_here = lax.dynamic_slice(
        block_mask, (row_index * blocks_here, col_index * sup_here), (blocks_here, sup_here)
    )
    keep_mask = jnp.repeat(jnp.repeat(mask_here, block_width, 0), block_width, 1).astype(
        jnp.bfloat16
    )
    masked = factor * keep_mask
    full_rows = whole_of(masked, COL, 1)
    row_ratio = lax.axis_size("row") // lax.axis_size(COL)
    row_pieces = []
    for offset in range(row_ratio):
        row_pieces.append(broadcast_by_parts(full_rows, "row", row_ratio * col_index + offset))
    summed = jnp.zeros((full_rows.shape[1], rows_here), jnp.float32)
    for offset in range(row_ratio):
        columns = row_pieces[offset]
        inverse_part = inverse_tiles[:, offset * rows_here : (offset + 1) * rows_here]
        summed = summed + lax.dot_general(
            columns, inverse_part, (((0,), (1,)), ((), ())), preferred_element_type=jnp.float32
        )
    reduced = sum_by_axis(summed, COL, 0)
    left_factor = masked.astype(jnp.float32).reshape(rows_here, sup_here, block_width)
    right_product = reduced.reshape(sup_here, block_width, rows_here)
    partial_diag = jnp.einsum(
        "jbr,rja->jab", right_product, left_factor, precision=lax.Precision.HIGHEST
    )
    summed_diag = taken_together(partial_diag.astype(jnp.bfloat16), "row").astype(jnp.float32)
    own_diag = lax.dynamic_slice_in_dim(diag_inverse, col_index * sup_here, sup_here, 0)
    return ((-reduced).astype(jnp.bfloat16), own_diag + summed_diag)


def solution(mesh):
    finer = Mesh(mesh.devices.reshape(mesh.shape["row"], 4, 2), ("row", "col_0", "col_1"))
    in_specs = (P("row", COL), P("row", COL), P(), P())
    out_specs = (P(COL, "row"), P(COL, None, None))
    return jax.shard_map(
        per_device, mesh=finer, in_specs=in_specs, out_specs=out_specs, check_vma=False
    )
```

profile of v0, /device:TPU:1, one launch (start us, length us, event | category | flops | bytes accessed | tf_op | source)
XLA Modules:
  0.0 650.2 jit_solution(2144273733660245835)
XLA Ops:
  7.2 0.0 all-gather.5.cloned.1.call-start
  7.2 0.8 dynamic-slice_convert_fusion
  8.0 0.1 copy.8
  8.1 0.1 broadcast_in_dim.12
  8.2 1.9 broadcast_in_dim.13
  10.1 2.1 bitcast_multiply_fusion
  12.2 0.0 all-gather.5.cloned.1.call-update
  12.3 0.0 all-gather.7.cloned.1.call-start
  12.3 33.0 %all-gather.5.cloned.1.call-done = bf16[1536,512]{1,0:T(8,128)(2,1)} async-done(((bf16[1536,256]{1,0:T(8,128)(2,1)}), bf16[1536,512]{1,0:T(8,128)(2,1)}) %all-gather.5.cloned.1.call-update) | async-done | bytes 1572880 | tf_op jit(solution)/shard_map/all_gather | solution.py:12
  45.3 0.0 all-gather.7.cloned.1.call-update
  45.3 0.0 reduce-scatter.5.cloned.1.call-start
  45.4 68.2 %all-gather.7.cloned.1.call-done = bf16[1536,2048]{1,0:T(8,128)(2,1)} async-done(((bf16[1536,512]{1,0:T(8,128)(2,1)}), bf16[1536,2048]{1,0:T(8,128)(2,1)}) %all-gather.7.cloned.1.call-update) | async-done | bytes 6291472 | tf_op jit(solution)/shard_map/all_gather | solution.py:12
  113.6 8.2 %broadcast_select_fusion = (bf16[1536,2048]{1,0:T(8,128)(2,1)}, bf16[1536,2048]{1,0:T(8,128)(2,1)}) fusion(bf16[1536,2048]{1,0:T(8,128)(2,1)} %all-gather.7.cloned.1.call-done, pred[]{:T(512)S(6)} %eq.7, pred[]{:T(512)S(6)} %eq.6), kind=kLoop, calls=%fused_computation.1 | loop fusion | flops 6291456 | bytes 18874370 | tf_op jit(solution)/shard_map/jit(_where)/select_n | solution.py:24
  121.8 0.0 reduce-scatter.5.cloned.1.call-update
  121.8 0.0 reduce-scatter.7.cloned.1.call-start
  121.8 0.5 reduce-scatter.7.cloned.1.call-update
  122.4 0.0 all-gather.9.cloned.1.call-start
  122.4 88.9 %reduce-scatter.5.cloned.1.call-done = bf16[96,2048]{1,0:T(8,128)(2,1)} async-done(((bf16[1536,2048]{1,0:T(8,128)(2,1)}), bf16[96,2048]{1,0:T(8,128)(2,1)}) %reduce-scatter.5.cloned.1.call-update) | async-done | bytes 393232 | tf_op jit(solution)/shard_map/reduce_scatter | solution.py:28
  211.3 0.0 all-gather.9.cloned.1.call-update
  211.4 0.0 all-gather.11.cloned.1.call-start
  211.4 93.1 %reduce-scatter.7.cloned.1.call-done = bf16[96,2048]{1,0:T(8,128)(2,1)} async-done(((bf16[1536,2048]{1,0:T(8,128)(2,1)}), bf16[96,2048]{1,0:T(8,128)(2,1)}) %reduce-scatter.7.cloned.1.call-update) | async-done | bytes 393232 | tf_op jit(solution)/shard_map/reduce_scatter | solution.py:28
  304.5 0.0 all-gather.11.cloned.1.call-update
  304.6 0.0 reduce-scatter.9.cloned.1.call-start
  304.6 66.8 %all-gather.9.cloned.1.call-done = bf16[1536,2048]{1,0:T(8,128)(2,1)} async-done(((bf16[96,2048]{1,0:T(8,128)(2,1)}), bf16[1536,2048]{1,0:T(8,128)(2,1)}) %all-gather.9.cloned.1.call-update) | async-done | bytes 6291472 | tf_op jit(solution)/shard_map/all_gather | solution.py:29
  371.4 16.1 %fusion.1 = f32[2048,1536]{1,0:T(8,128)} fusion(bf16[1536,2048]{1,0:T(8,128)(2,1)} %all-gather.9.cloned.1.call-done, bf16[1536,3072]{1,0:T(8,128)(2,1)} %param.4), kind=kOutput, calls=%fused_computation.4 | convolution fusion | flops 9663676416 | bytes 23592960 | tf_op jit(solution)/shard_map/dot_general | solution.py:71
  387.5 48.2 %all-gather.11.cloned.1.call-done = bf16[1536,2048]{1,0:T(8,128)(2,1)} async-done(((bf16[96,2048]{1,0:T(8,128)(2,1)}), bf16[1536,2048]{1,0:T(8,128)(2,1)}) %all-gather.11.cloned.1.call-update) | async-done | bytes 6291472 | tf_op jit(solution)/shard_map/all_gather | solution.py:29
  435.7 17.9 %convolution_add_fusion = f32[2048,1536]{1,0:T(8,128)} fusion(f32[2048,1536]{1,0:T(8,128)} %fusion.1, bf16[1536,2048]{1,0:T(8,128)(2,1)} %all-gather.11.cloned.1.call-done, bf16[1536,3072]{1,0:T(8,128)(2,1)} %param.4), kind=kOutput, calls=%fused_computation | convolution fusion | flops 9666822144 | bytes 36175872 | tf_op jit(solution)/shard_map/dot_general | solution.py:71
  453.6 0.0 copy-start
  453.6 0.0 reduce-scatter.9.cloned.1.call-update
  453.7 0.0 reduce-scatter.11.cloned.1.call-start
  453.7 111.8 %reduce-scatter.9.cloned.1.call-done = f32[512,1536]{1,0:T(8,128)} async-done(((f32[2048,1536]{1,0:T(8,128)}), f32[512,1536]{1,0:T(8,128)}) %reduce-scatter.9.cloned.1.call-update) | async-done | bytes 3145744 | tf_op jit(solution)/shard_map/reduce_scatter | solution.py:35
  565.6 0.0 reduce-scatter.11.cloned.1.call-update
  565.6 0.0 copy-done
  565.6 0.3 copy.10
  565.9 47.6 %reduce-scatter.11.cloned.1.call-done = f32[256,1536]{1,0:T(8,128)} async-done(((f32[512,1536]{1,0:T(8,128)}), f32[256,1536]{1,0:T(8,128)}) %reduce-scatter.11.cloned.1.call-update) | async-done | bytes 1572880 | tf_op jit(solution)/shard_map/reduce_scatter | solution.py:35
  613.5 0.0 copy-start.1
  613.5 2.4 convolution_convert_fusion
  616.0 1.2 broadcast_in_dim.14
  617.2 7.3 %all-to-all-start = ((bf16[16,2,128,128]{3,2,1,0:T(8,128)(2,1)}), bf16[16,2,128,128]{3,2,1,0:T(8,128)(2,1)S(1)}, u32[]{:S(2)}, u32[]{:S(2)}) async-start(bf16[16,2,128,128]{3,2,1,0:T(8,128)(2,1)} %broadcast_in_dim.14), calls=%async_computation.4 | async-start | bytes 2097152 | tf_op jit(solution)/shard_map/all_to_all | solution.py:41
  624.4 0.0 copy-done.1
  624.5 1.0 negate_convert_fusion
  625.4 16.2 %all-to-all-done = bf16[16,2,128,128]{3,2,1,0:T(8,128)(2,1)S(1)} async-done(((bf16[16,2,128,128]{3,2,1,0:T(8,128)(2,1)}), bf16[16,2,128,128]{3,2,1,0:T(8,128)(2,1)S(1)}, u32[]{:S(2)}, u32[]{:S(2)}) %all-to-all-start) | async-done | bytes 1048608 | tf_op jit(solution)/shard_map/all_to_all | solution.py:41
  641.7 0.1 convert_reduce_fusion
  641.8 1.6 dynamic-slice_add_fusion
Async XLA Ops:
  7.2 38.1 %all-gather.5.cloned.1.call-start = ((), (), s32[]{:S(2)}) async-start(), calls=%async_computation.5 | async-start | bytes 2359296 | tf_op jit(solution)/shard_map/all_gather | solution.py:12
  12.3 101.3 %all-gather.7.cloned.1.call-start = ((), (), s32[]{:S(2)}) async-start(), calls=%async_computation.6 | async-start | bytes 7864320 | tf_op jit(solution)/shard_map/all_gather | solution.py:12
  45.3 166.0 %reduce-scatter.5.cloned.1.call-start = ((), (), s32[]{:S(2)}) async-start(), calls=%async_computation.7 | async-start | bytes 6684672 | tf_op jit(solution)/shard_map/reduce_scatter | solution.py:28
  121.8 182.8 %reduce-scatter.7.cloned.1.call-start = ((), (), s32[]{:S(2)}) async-start(), calls=%async_computation.9 | async-start | bytes 6684672 | tf_op jit(solution)/shard_map/reduce_scatter | solution.py:28
  122.4 249.1 %all-gather.9.cloned.1.call-start = ((), (), s32[]{:S(2)}) async-start(), calls=%async_computation.8 | async-start | bytes 6684672 | tf_op jit(solution)/shard_map/all_gather | solution.py:29
  211.4 224.4 %all-gather.11.cloned.1.call-start = ((), (), s32[]{:S(2)}) async-start(), calls=%async_computation.10 | async-start | bytes 6684672 | tf_op jit(solution)/shard_map/all_gather | solution.py:29
  304.6 261.0 %reduce-scatter.9.cloned.1.call-start = ((), (), s32[]{:S(2)}) async-start(), calls=%async_computation.11 | async-start | bytes 15728640 | tf_op jit(solution)/shard_map/reduce_scatter | solution.py:35
  453.6 112.0 %copy-start = (bf16[1536,256]{1,0:T(8,128)(2,1)S(1)}, bf16[1536,256]{1,0:T(8,128)(2,1)}, u32[]{:S(2)}) copy-start(bf16[1536,256]{1,0:T(8,128)(2,1)} %bitcast_multiply_fusion) | copy-start | bytes 2359300
  453.7 159.8 %reduce-scatter.11.cloned.1.call-start = ((), (), s32[]{:S(2)}) async-start(), calls=%async_computation.12 | async-start | bytes 4718592 | tf_op jit(solution)/shard_map/reduce_scatter | solution.py:35
  613.5 10.9 %copy-start.1 = (f32[256,1536]{1,0:T(8,128)S(1)}, f32[256,1536]{1,0:T(8,128)}, u32[]{:S(2)}) copy-start(f32[256,1536]{1,0:T(8,128)} %reduce-scatter.11.cloned.1.call-done) | copy-start | bytes 4718596
  617.2 24.5 %all-to-all-start = ((bf16[16,2,128,128]{3,2,1,0:T(8,128)(2,1)}), bf16[16,2,128,128]{3,2,1,0:T(8,128)(2,1)S(1)}, u32[]{:S(2)}, u32[]{:S(2)}) async-start(bf16[16,2,128,128]{3,2,1,0:T(8,128)(2,1)} %broadcast_in_dim.14), calls=%async_computation.4 | async-start | bytes 2097152 | tf_op jit(solution)/shard_map/all_to_all | solution.py:41
Sparse Core Ops, SparseCore 0:
  12.4 32.8 all-gather.4
  47.0 66.5 all-gather.6
  121.9 89.3 reduce-scatter.4
  216.0 88.5 reduce-scatter.6
  306.8 64.5 all-gather.8
  373.8 61.9 all-gather.10
  453.8 111.7 reduce-scatter.8
  567.9 45.5 reduce-scatter.10
where the time goes:
time: 651 us; the launch traced here: 650 us
  waiting for transfers between devices  575 us (88%)
  matrix products  36.4 us (6%)
  between operations  14.2 us (2%)
  other arithmetic  13.8 us (2%)
  starting transfers between devices  7.6 us (1%)
    reduce_scatter x2, waiting for transfers between devices, broadcast_by_parts(): own = lax.psum_scatter(padded, axis, scatter_dimension=0, tiled=True)  182 us
    reduce_scatter x2, waiting for transfers between devices, sum_by_axis(): nearer = lax.psum_scatter(x, axes[0], scatter_dimension=dim, tiled=True)  159 us
    all_gather x2, waiting for transfers between devices, broadcast_by_parts(): lax.all_gather(own, axis, axis=0, tiled=True)[:len(lines)].reshape(x.shape)  115 us
    all_gather x2, waiting for transfers between devices, whole_of(): x = lax.all_gather(x, axis, axis=dim, tiled=True)  101 us
    dot_general x2, matrix products, per_device(): lax.dot_general(columns, inverse_part, (((0,), (1,)), ((), ())), preferre...  34 us
    all_to_all x1, waiting for transfers between devices, sent_to_all(): lax.all_to_all(jnp.broadcast_to(x[None], (length, *x.shape)), axis, 0, 0,...  16.2 us
  transfers between devices with their start and end apart: 9, of which 9 were waited for; matrix products, arithmetic and copies ran while one was open for 3% of the time, Pallas kernels for 0%

commit v1 on v0

--- a/solution.py
+++ b/solution.py
@@ -26,7 +26,9 @@
     )
     padded = filled_up(lines, lax.axis_size(axis))
     own = lax.psum_scatter(padded, axis, scatter_dimension=0, tiled=True)
-    return lax.all_gather(own, axis, axis=0, tiled=True)[: len(lines)].reshape(x.shape)
+    return jnp.concatenate(
+        lax.all_to_all(jnp.stack([own] * lax.axis_size(axis)), axis, 0, 0), axis=0
+    )[: len(lines)].reshape(x.shape)
 
 
 def sum_by_axis(x, axes, dim):

time: 651 us -> 631 us (0.969)
  waiting for transfers between devices: 575 us -> 534 us
  starting transfers between devices: 7.6 us -> 20.1 us
  local copies, waits for them, and re-layouts: 3.59 us -> 12.5 us
    all_gather x2 -> x0, waiting for transfers between devices: 115 us -> none  [broadcast_by_parts(): lax.all_gather(own, axis, axis=0, tiled=True)[:len(lines)].reshape(x.shape)]
    all_to_all x0 -> x2, waiting for transfers between devices: none -> 57.3 us  [broadcast_by_parts(): lax.all_to_all(jnp.stack([own] * lax.axis_size(axis)), axis, 0, 0)]
    reduce_scatter x2, waiting for transfers between devices: 182 us -> 199 us  [broadcast_by_parts(): own = lax.psum_scatter(padded, axis, scatter_dimension=0, tiled=True)]
    all_to_all x0 -> x2, starting transfers between devices: none -> 12.4 us  [broadcast_by_parts(): lax.all_to_all(jnp.stack([own] * lax.axis_size(axis)), axis, 0, 0)]
    another operation x0 -> x2, local copies, waits for them, and re-layouts: none -> 8.91 us  [broadcast_by_parts(): jnp.stack([own] * lax.axis_size(axis))]
  transfers between devices with their start and end apart: 9 -> 9, of which waited for: 9 -> 8; matrix products, arithmetic and copies ran while one was open for 3% -> 3% of each run, Pallas kernels for 0% -> 0%
where the time goes in v1:
time: 631 us
  waiting for transfers between devices  534 us (85%)
  matrix products  36.5 us (6%)
  starting transfers between devices  20.1 us (3%)
  between operations  14.2 us (2%)
  other arithmetic  13.7 us (2%)
  local copies, waits for them, and re-layouts  12.5 us (2%)
    reduce_scatter x2, waiting for transfers between devices, broadcast_by_parts(): own = lax.psum_scatter(padded, axis, scatter_dimension=0, tiled=True)  199 us
    reduce_scatter x2, waiting for transfers between devices, sum_by_axis(): nearer = lax.psum_scatter(x, axes[0], scatter_dimension=dim, tiled=True)  160 us
    all_gather x2, waiting for transfers between devices, whole_of(): x = lax.all_gather(x, axis, axis=dim, tiled=True)  101 us
    all_to_all x2, waiting for transfers between devices, broadcast_by_parts(): lax.all_to_all(jnp.stack([own] * lax.axis_size(axis)), axis, 0, 0)  57.3 us
    dot_general x2, matrix products, per_device(): lax.dot_general(columns, inverse_part, (((0,), (1,)), ((), ())), preferre...  34.1 us
    all_to_all x1, waiting for transfers between devices, sent_to_all(): lax.all_to_all(jnp.broadcast_to(x[None], (length, *x.shape)), axis, 0, 0,...  16.2 us
  transfers between devices with their start and end apart: 9, of which 8 were waited for; matrix products, arithmetic and copies ran while one was open for 3% of the time, Pallas kernels for 0%

profile of v1, /device:TPU:1, one launch (start us, length us, event | category | flops | bytes accessed | tf_op | source)
XLA Modules:
  0.0 630.6 jit_solution(10231004914871061939)
XLA Ops:
  7.2 0.0 all-gather.3.cloned.1.call-start
  7.2 0.8 dynamic-slice_convert_fusion
  8.0 0.1 copy.8
  8.1 0.1 broadcast_in_dim.12
  8.2 1.9 broadcast_in_dim.13
  10.1 2.1 bitcast_multiply_fusion
  12.2 0.0 all-gather.3.cloned.1.call-update
  12.3 0.0 all-gather.5.cloned.1.call-start
  12.3 33.0 %all-gather.3.cloned.1.call-done = bf16[1536,512]{1,0:T(8,128)(2,1)} async-done(((bf16[1536,256]{1,0:T(8,128)(2,1)}), bf16[1536,512]{1,0:T(8,128)(2,1)}) %all-gather.3.cloned.1.call-update) | async-done | bytes 1572880 | tf_op jit(solution)/shard_map/all_gather | solution.py:12
  45.3 0.0 all-gather.5.cloned.1.call-update
  45.3 0.0 reduce-scatter.5.cloned.1.call-start
  45.4 68.2 %all-gather.5.cloned.1.call-done = bf16[1536,2048]{1,0:T(8,128)(2,1)} async-done(((bf16[1536,512]{1,0:T(8,128)(2,1)}), bf16[1536,2048]{1,0:T(8,128)(2,1)}) %all-gather.5.cloned.1.call-update) | async-done | bytes 6291472 | tf_op jit(solution)/shard_map/all_gather | solution.py:12
  113.6 8.1 %broadcast_select_fusion = (bf16[1536,2048]{1,0:T(8,128)(2,1)}, bf16[1536,2048]{1,0:T(8,128)(2,1)}) fusion(bf16[1536,2048]{1,0:T(8,128)(2,1)} %all-gather.5.cloned.1.call-done, pred[]{:T(512)S(6)} %eq.7, pred[]{:T(512)S(6)} %eq.6), kind=kLoop, calls=%fused_computation.1 | loop fusion | flops 6291456 | bytes 18874370 | tf_op jit(solution)/shard_map/jit(_where)/select_n | solution.py:24
  121.7 0.0 reduce-scatter.5.cloned.1.call-update
  121.7 0.0 reduce-scatter.7.cloned.1.call-start
  121.8 0.5 reduce-scatter.7.cloned.1.call-update
  122.3 89.0 %reduce-scatter.5.cloned.1.call-done = bf16[96,2048]{1,0:T(8,128)(2,1)} async-done(((bf16[1536,2048]{1,0:T(8,128)(2,1)}), bf16[96,2048]{1,0:T(8,128)(2,1)}) %reduce-scatter.5.cloned.1.call-update) | async-done | bytes 393232 | tf_op jit(solution)/shard_map/reduce_scatter | solution.py:28
  211.3 4.4 stack.4
  215.7 6.2 all-to-all-start
  221.9 109.6 %reduce-scatter.7.cloned.1.call-done = bf16[96,2048]{1,0:T(8,128)(2,1)} async-done(((bf16[1536,2048]{1,0:T(8,128)(2,1)}), bf16[96,2048]{1,0:T(8,128)(2,1)}) %reduce-scatter.7.cloned.1.call-update) | async-done | bytes 393232 | tf_op jit(solution)/shard_map/reduce_scatter | solution.py:28
  331.5 0.0 all-to-all-done
  331.5 4.5 stack.5
  336.0 6.2 all-to-all-start.1
  342.2 0.2 reduce-scatter.9.cloned.1.call-start
  342.4 16.1 %fusion.1 = f32[2048,1536]{1,0:T(8,128)} fusion(bf16[1536,2048]{1,0:T(8,128)(2,1)} %bitcast.1, bf16[1536,3072]{1,0:T(8,128)(2,1)} %param.4), kind=kOutput, calls=%fused_computation.4 | convolution fusion | flops 9663676416 | bytes 23592960 | tf_op jit(solution)/shard_map/dot_general | solution.py:73
  358.5 57.3 %all-to-all-done.1 = bf16[16,96,2048]{2,1,0:T(8,128)(2,1)} async-done(((bf16[16,96,2048]{2,1,0:T(8,128)(2,1)}), bf16[16,96,2048]{2,1,0:T(8,128)(2,1)}, u32[]{:S(2)}, u32[]{:S(2)}) %all-to-all-start.1) | async-done | bytes 6291488 | tf_op jit(solution)/shard_map/all_to_all | solution.py:30
  415.8 17.9 %convolution_add_fusion = f32[2048,1536]{1,0:T(8,128)} fusion(f32[2048,1536]{1,0:T(8,128)} %fusion.1, bf16[1536,2048]{1,0:T(8,128)(2,1)} %bitcast.2, bf16[1536,3072]{1,0:T(8,128)(2,1)} %param.4), kind=kOutput, calls=%fused_computation | convolution fusion | flops 9666822144 | bytes 36175872 | tf_op jit(solution)/shard_map/dot_general | solution.py:73
  433.7 0.0 copy-start
  433.7 0.0 reduce-scatter.9.cloned.1.call-update
  433.8 0.0 reduce-scatter.11.cloned.1.call-start
  433.8 112.3 %reduce-scatter.9.cloned.1.call-done = f32[512,1536]{1,0:T(8,128)} async-done(((f32[2048,1536]{1,0:T(8,128)}), f32[512,1536]{1,0:T(8,128)}) %reduce-scatter.9.cloned.1.call-update) | async-done | bytes 3145744 | tf_op jit(solution)/shard_map/reduce_scatter | solution.py:37
  546.1 0.0 reduce-scatter.11.cloned.1.call-update
  546.1 0.0 copy-done
  546.2 0.3 copy.10
  546.4 47.5 %reduce-scatter.11.cloned.1.call-done = f32[256,1536]{1,0:T(8,128)} async-done(((f32[512,1536]{1,0:T(8,128)}), f32[256,1536]{1,0:T(8,128)}) %reduce-scatter.11.cloned.1.call-update) | async-done | bytes 1572880 | tf_op jit(solution)/shard_map/reduce_scatter | solution.py:37
  593.9 0.0 copy-start.1
  593.9 2.4 convolution_convert_fusion
  596.4 1.2 broadcast_in_dim.14
  597.6 7.3 %all-to-all-start.2 = ((bf16[16,2,128,128]{3,2,1,0:T(8,128)(2,1)}), bf16[16,2,128,128]{3,2,1,0:T(8,128)(2,1)S(1)}, u32[]{:S(2)}, u32[]{:S(2)}) async-start(bf16[16,2,128,128]{3,2,1,0:T(8,128)(2,1)} %broadcast_in_dim.14), calls=%async_computation.6 | async-start | bytes 2097152 | tf_op jit(solution)/shard_map/all_to_all | solution.py:43
  604.9 0.0 copy-done.1
  604.9 1.0 negate_convert_fusion
  605.8 16.2 %all-to-all-done.2 = bf16[16,2,128,128]{3,2,1,0:T(8,128)(2,1)S(1)} async-done(((bf16[16,2,128,128]{3,2,1,0:T(8,128)(2,1)}), bf16[16,2,128,128]{3,2,1,0:T(8,128)(2,1)S(1)}, u32[]{:S(2)}, u32[]{:S(2)}) %all-to-all-start.2) | async-done | bytes 1048608 | tf_op jit(solution)/shard_map/all_to_all | solution.py:43
  622.1 0.1 convert_reduce_fusion
  622.2 1.6 dynamic-slice_add_fusion
Async XLA Ops:
  7.2 38.1 %all-gather.3.cloned.1.call-start = ((), (), s32[]{:S(2)}) async-start(), calls=%async_computation.7 | async-start | bytes 2359296 | tf_op jit(solution)/shard_map/all_gather | solution.py:12
  12.3 101.3 %all-gather.5.cloned.1.call-start = ((), (), s32[]{:S(2)}) async-start(), calls=%async_computation.8 | async-start | bytes 7864320 | tf_op jit(solution)/shard_map/all_gather | solution.py:12
  45.3 166.0 %reduce-scatter.5.cloned.1.call-start = ((), (), s32[]{:S(2)}) async-start(), calls=%async_computation.9 | async-start | bytes 6684672 | tf_op jit(solution)/shard_map/reduce_scatter | solution.py:28
  121.7 209.7 %reduce-scatter.7.cloned.1.call-start = ((), (), s32[]{:S(2)}) async-start(), calls=%async_computation.10 | async-start | bytes 6684672 | tf_op jit(solution)/shard_map/reduce_scatter | solution.py:28
  215.7 115.7 %all-to-all-start = ((bf16[16,96,2048]{2,1,0:T(8,128)(2,1)}), bf16[16,96,2048]{2,1,0:T(8,128)(2,1)}, u32[]{:S(2)}, u32[]{:S(2)}) async-start(bf16[16,96,2048]{2,1,0:T(8,128)(2,1)} %stack.4), calls=%async_computation.1 | async-start | bytes 12582912 | tf_op jit(solution)/shard_map/all_to_all | solution.py:30
  336.0 79.9 %all-to-all-start.1 = ((bf16[16,96,2048]{2,1,0:T(8,128)(2,1)}), bf16[16,96,2048]{2,1,0:T(8,128)(2,1)}, u32[]{:S(2)}, u32[]{:S(2)}) async-start(bf16[16,96,2048]{2,1,0:T(8,128)(2,1)} %stack.5), calls=%async_computation.3 | async-start | bytes 12582912 | tf_op jit(solution)/shard_map/all_to_all | solution.py:30
  342.2 203.9 %reduce-scatter.9.cloned.1.call-start = ((), (), s32[]{:S(2)}) async-start(), calls=%async_computation.11 | async-start | bytes 15728640 | tf_op jit(solution)/shard_map/reduce_scatter | solution.py:37
  433.7 112.4 %copy-start = (bf16[1536,256]{1,0:T(8,128)(2,1)S(1)}, bf16[1536,256]{1,0:T(8,128)(2,1)}, u32[]{:S(2)}) copy-start(bf16[1536,256]{1,0:T(8,128)(2,1)} %bitcast_multiply_fusion) | copy-start | bytes 2359300
  433.8 160.1 %reduce-scatter.11.cloned.1.call-start = ((), (), s32[]{:S(2)}) async-start(), calls=%async_computation.12 | async-start | bytes 4718592 | tf_op jit(solution)/shard_map/reduce_scatter | solution.py:37
  593.9 10.9 %copy-start.1 = (f32[256,1536]{1,0:T(8,128)S(1)}, f32[256,1536]{1,0:T(8,128)}, u32[]{:S(2)}) copy-start(f32[256,1536]{1,0:T(8,128)} %reduce-scatter.11.cloned.1.call-done) | copy-start | bytes 4718596
  597.6 24.5 %all-to-all-start.2 = ((bf16[16,2,128,128]{3,2,1,0:T(8,128)(2,1)}), bf16[16,2,128,128]{3,2,1,0:T(8,128)(2,1)S(1)}, u32[]{:S(2)}, u32[]{:S(2)}) async-start(bf16[16,2,128,128]{3,2,1,0:T(8,128)(2,1)} %broadcast_in_dim.14), calls=%async_computation.6 | async-start | bytes 2097152 | tf_op jit(solution)/shard_map/all_to_all | solution.py:43
Sparse Core Ops, SparseCore 0:
  12.4 32.8 all-gather.2
  47.0 66.5 all-gather.4
  121.9 89.3 reduce-scatter.4
  215.9 115.5 reduce-scatter.6
  433.9 112.1 reduce-scatter.8
  548.3 45.5 reduce-scatter.10
